TPU v7x, 256 devices: a whole 4x4x8 slice. The times are simulated.
256 devices in a mesh: dp: 16 (over z, x_hi), ctx: 16 (over x_lo, y, core).
Axes of the slice: x: 4 (x_hi: 2, x_lo: 2; x = x_hi * 2 + x_lo), y: 4, z: 8, core: 2. Of those that a mesh axis runs over, the one named last changes fastest.
Arguments:
- features: bfloat16 [16, 8192, 768], P('dp', 'ctx'), may hold values from -24 to 24
- bases: int32 [16, 8192], P('dp', 'ctx'), may hold values from 0 to 3
- dna_table: bfloat16 [4, 768], replicated, may hold values from -6 to 6
- norm_gain: bfloat16 [768], replicated, may hold values from 0.099609375 to 1.8984375
- w_conv: bfloat16 [5, 768, 768], replicated, may hold values from -0.09375 to 0.09375
- w_query: bfloat16 [768, 768], replicated, may hold values from -0.21875 to 0.21875
- w_key: bfloat16 [768, 768], replicated, may hold values from -0.21875 to 0.21875
- w_value: bfloat16 [768, 768], replicated, may hold values from -0.21875 to 0.21875
- w_out: bfloat16 [768, 768], replicated, may hold values from -0.21875 to 0.21875
- cotangent: bfloat16 [16, 512, 768], P('dp', 'ctx'), may hold values from -48 to 48
Outputs:
- grad_features: bfloat16 [16, 8192, 768], P('dp', 'ctx')
- grad_conv: float32 [768, 5, 768], P('ctx', None, 'dp')
All inputs are finite; a program needn't handle non-finite values.
Results may differ from a plain program's by a relative error of at most 0.025.
The roundings to bfloat16 on the way count: a program that leaves them out, or rounds other values in their place, can miss the bound.
Values may be sent and summed in bfloat16 or wider, within the bound.
A program may use at most 128 MiB of HBM per device.

v0:
```python
import jax
import jax.numpy as jnp
from jax import lax
from jax.sharding import PartitionSpec as P

HEADS = 6
DH = 128
EPSILON = 1e-06
GELU_SCALE = 0.7978845608028654
CUBIC = 0.044715


def extended(block, sides, width):
    for axis, dim in sides:
        count = lax.axis_size(axis)
        forward = [(i, i + 1) for i in range(count - 1)]
        backward = [(target, source) for source, target in forward]
        low = lax.ppermute(
            lax.slice_in_dim(block, block.shape[dim] - width, None, axis=dim), axis, forward
        )
        high = lax.ppermute(lax.slice_in_dim(block, 0, width, axis=dim), axis, backward)
        block = jnp.concatenate([low, block, high], axis=dim)
    return block


def gelu_pair(inputs):
    inner = GELU_SCALE * (inputs + CUBIC * inputs**3)
    tanh_val = jnp.tanh(inner)
    values = 0.5 * inputs * (1.0 + tanh_val)
    slopes = 0.5 * (1.0 + tanh_val) + 0.5 * inputs * (1.0 - tanh_val**2) * GELU_SCALE * (
        1.0 + 3.0 * CUBIC * inputs**2
    )
    return (values, slopes)


def heads_split(matrix):
    return matrix.reshape(matrix.shape[0], HEADS, DH)


def dot_right_t(left, right):
    return lax.dot_general(
        left, right, (((1,), (1,)), ((), ())), preferred_element_type=jnp.float32
    )


def dot_left_t(left, right):
    return lax.dot_general(
        left, right, (((0,), (0,)), ((), ())), preferred_element_type=jnp.float32
    )


def per_device(
    features, bases, dna_table, norm_gain, w_conv, w_query, w_key, w_value, w_out, cotangent
):
    seg_feat = features[0]
    seg_base = bases[0]
    seg_cot = cotangent[0]
    kernel = w_conv.shape[0]
    half_width = kernel // 2
    length = seg_feat.shape[0]
    channels = seg_feat.shape[1]
    tok_rows = seg_cot.shape[0]
    onehot = (seg_base[:, None] == jnp.arange(4, dtype=jnp.int32)[None, :]).astype(jnp.bfloat16)
    summed_in = seg_feat.astype(jnp.float32) + jnp.dot(
        onehot, dna_table, preferred_element_type=jnp.float32
    )
    inv_rms = lax.rsqrt(jnp.mean(summed_in * summed_in, axis=-1, keepdims=True) + EPSILON)
    normed = summed_in * inv_rms
    gain_f = norm_gain.astype(jnp.float32)
    pre_gelu = normed * gain_f
    gelu_val, slopes = gelu_pair(pre_gelu)
    act = gelu_val.astype(jnp.bfloat16)
    rimmed = extended(act[None], (("ctx", 1),), half_width)[0]
    conv = jnp.zeros((length, channels), jnp.float32)
    for offset in range(kernel):
        conv = conv + jnp.dot(
            rimmed[offset : offset + length], w_conv[offset], preferred_element_type=jnp.float32
        )
    resid = summed_in + conv
    pooled = resid.reshape(tok_rows, -1, channels).mean(axis=1).astype(jnp.bfloat16)
    queries = jnp.dot(pooled, w_query, preferred_element_type=jnp.float32).astype(jnp.bfloat16)
    keys_local = jnp.dot(pooled, w_key, preferred_element_type=jnp.float32).astype(jnp.bfloat16)
    values_local = jnp.dot(pooled, w_value, preferred_element_type=jnp.float32).astype(jnp.bfloat16)
    keys_all, values_all = (
        lax.all_gather(keys_local, "ctx", axis=0, tiled=True),
        lax.all_gather(values_local, "ctx", axis=0, tiled=True),
    )
    scale = 1.0 / DH**0.5
    query_heads = heads_split(queries)
    key_heads = heads_split(keys_all)
    value_heads = heads_split(values_all)
    scores = (
        jnp.einsum("qhd,khd->hqk", query_heads, key_heads, preferred_element_type=jnp.float32)
        * scale
    )
    row_max = jnp.max(scores, axis=-1, keepdims=True)
    expo = jnp.exp(scores - row_max)
    row_total = jnp.sum(expo, axis=-1, keepdims=True)
    probs = expo / row_total
    probs_b = probs.astype(jnp.bfloat16)
    attn_out = jnp.einsum("hqk,khd->qhd", probs_b, value_heads, preferred_element_type=jnp.float32)
    attn_out = attn_out.reshape(tok_rows, channels).astype(jnp.bfloat16)
    grad_attn = dot_right_t(seg_cot, w_out).astype(jnp.bfloat16)
    grad_heads = heads_split(grad_attn)
    grad_prob = jnp.einsum(
        "qhd,khd->hqk", grad_heads, value_heads, preferred_element_type=jnp.float32
    )
    delta_rows = jnp.sum(
        grad_heads.astype(jnp.float32) * heads_split(attn_out).astype(jnp.float32), axis=-1
    )
    row_delta = delta_rows.transpose(1, 0)[:, :, None]
    grad_score = (probs * (grad_prob - row_delta) * scale).astype(jnp.bfloat16)
    grad_q = jnp.einsum("hqk,khd->qhd", grad_score, key_heads, preferred_element_type=jnp.float32)
    grad_q = grad_q.reshape(tok_rows, channels).astype(jnp.bfloat16)
    term_k = jnp.einsum("hqk,qhd->khd", grad_score, query_heads, preferred_element_type=jnp.float32)
    term_v = jnp.einsum("hqk,qhd->khd", probs_b, grad_heads, preferred_element_type=jnp.float32)
    summed_kv = lax.psum_scatter(
        jnp.concatenate(
            (
                term_k.reshape(lax.axis_size("ctx") * tok_rows, channels),
                term_v.reshape(lax.axis_size("ctx") * tok_rows, channels),
            ),
            axis=1,
        ),
        "ctx",
        scatter_dimension=0,
        tiled=True,
    )
    grad_k = summed_kv[:, :channels].astype(jnp.bfloat16)
    grad_v = summed_kv[:, channels:].astype(jnp.bfloat16)
    grad_pooled = (
        seg_cot.astype(jnp.float32)
        + dot_right_t(grad_q, w_query)
        + dot_right_t(grad_k, w_key)
        + dot_right_t(grad_v, w_value)
    )
    pool_size = length // tok_rows
    grad_rows = jnp.repeat((grad_pooled / pool_size).astype(jnp.bfloat16), pool_size, axis=0)
    grad_pad = extended(grad_rows[None], (("ctx", 1),), half_width)[0]
    grad_act = jnp.zeros((length, channels), jnp.float32)
    for offset in range(kernel):
        begin = 2 * half_width - offset
        grad_act = grad_act + dot_right_t(grad_pad[begin : begin + length], w_conv[offset])
    windows = jnp.stack(
        [rimmed[offset : offset + length] for offset in range(kernel)], axis=2
    ).reshape(length, channels * kernel)
    factor = 1.0 / (lax.axis_size("dp") * length * lax.axis_size("ctx")) ** 0.5
    whole_terms = (dot_left_t(windows, grad_rows) * factor).reshape(channels, kernel, channels)
    shared = lax.psum_scatter(whole_terms, "ctx", scatter_dimension=0, tiled=True)
    grad_conv = lax.psum_scatter(shared, "dp", scatter_dimension=2, tiled=True)
    grad_norm = grad_act * slopes * gain_f
    grad_in = grad_rows.astype(jnp.float32) + inv_rms * (
        grad_norm - normed * jnp.mean(grad_norm * normed, axis=-1, keepdims=True)
    )
    return (grad_in.astype(jnp.bfloat16)[None], grad_conv)


def solution(mesh):
    in_specs = (
        P("dp", "ctx", None),
        P("dp", "ctx"),
        P(),
        P(),
        P(),
        P(),
        P(),
        P(),
        P(),
        P("dp", "ctx", None),
    )
    out_specs = (P("dp", "ctx", None), P("ctx", None, "dp"))
    return jax.shard_map(
        per_device, mesh=mesh, in_specs=in_specs, out_specs=out_specs, check_vma=False
    )
```

profile of v0, /device:TPU:8, one launch (start us, length us, event | category | flops | bytes accessed | tf_op | source)
XLA Modules:
  0.0 533.8 jit_solution(988875582411830763)
XLA Ops:
  7.2 0.0 reduce-scatter.10.cloned.1.call-start
  7.2 0.8 convert_element_type.74
  8.0 1.7 multiply_reduce_fusion.1
  9.7 0.7 fusion.122
  10.4 1.9 collective-permute-start
  12.3 3.9 collective-permute-start.1
  16.2 2.5 fusion.22
  18.8 1.1 fusion.40
  19.9 0.8 fusion.26
  20.7 0.8 fusion.30
  21.5 0.8 fusion.18
  22.3 1.1 bitcast_reduce_fusion
  23.4 0.9 fusion.39
  24.4 0.9 convolution_convert_fusion.2
  25.3 0.3 convolution_convert_fusion.5
  25.6 20.5 %all_gather.6 = bf16[512,768]{1,0:T(8,128)(2,1)} all-gather(bf16[32,768]{1,0:T(8,128)(2,1)S(1)} %convolution_convert_fusion.5), channel_id=1, replica_groups=mesh['dp'=16,'ctx'=16] {'ctx'}, dimensions={0}, use_global_device_ids=true | all-gather | bytes 835584 | tf_op jit(solution)/shard_map/all_gather | solution.py:85
  46.1 2.3 copy.36
  48.4 1.4 convolution_multiply_fusion.1
  49.8 0.8 copy-done.7
  50.6 0.9 fusion.100
  51.5 22.8 %all_gather.7 = bf16[512,768]{1,0:T(8,128)(2,1)} all-gather(bf16[32,768]{1,0:T(8,128)(2,1)S(1)} %copy-done.13), channel_id=1, replica_groups=mesh['dp'=16,'ctx'=16] {'ctx'}, dimensions={0}, use_global_device_ids=true | all-gather | bytes 835584 | tf_op jit(solution)/shard_map/all_gather | solution.py:86
  74.3 2.3 copy.39
  76.6 2.8 fusion.77
  79.5 2.4 fusion.38
  81.9 1.6 fusion.32
  83.6 0.7 copy-done.9
  84.2 0.4 fusion.80
  84.6 2.0 pad_maximum_fusion
  86.6 3.6 copy.54
  90.2 0.0 reduce-scatter.10.cloned.1.call-update
  90.2 0.2 reduce-scatter.8.cloned.1.call-start
  90.5 0.4 copy-done.15
  90.9 1.1 bitcast_dynamic-update-slice_fusion.4
  91.9 1.1 bitcast_dynamic-update-slice_fusion.3
  93.0 1.6 bitcast_dynamic-update-slice_fusion.2
  94.6 1.2 bitcast_dynamic-update-slice_fusion.1
  95.8 1.1 bitcast_dynamic-update-slice_fusion
  96.8 8.4 %copy.48 = bf16[512,768,5]{0,2,1:T(8,128)(2,1)} copy(bf16[512,768,5]{1,0,2:T(8,128)(2,1)} %bitcast_dynamic-update-slice_fusion) | data formatting | bytes 7864320 | tf_op jit(solution)/shard_map/stack | solution.py:144
  105.3 8.5 %reshape.82 = bf16[512,3840]{0,1:T(8,128)(2,1)} reshape(bf16[512,768,5]{0,2,1:T(8,128)(2,1)} %copy.48) | data formatting | bytes 7864320 | tf_op jit(solution)/shard_map/reshape | solution.py:146
  113.8 1.3 fusion.41
  115.1 1.3 convolution_add_fusion.2
  116.4 38.6 %reduce-scatter.10.cloned.1.call-done = f32[32,1536]{1,0:T(8,128)} async-done(((f32[512,1536]{1,0:T(8,128)}), f32[32,1536]{1,0:T(8,128)}) %reduce-scatter.10.cloned.1.call-update) | async-done | bytes 196624
  155.0 1.1 copy.55
  156.1 1.7 convolution_add_fusion.1
  157.9 0.0 copy-done.6
  157.9 0.5 fusion.34
  158.4 0.1 broadcast_in_dim.7
  158.5 9.7 %convolution_multiply_fusion = f32[3840,768]{1,0:T(8,128)} fusion(bf16[512,3840]{0,1:T(8,128)(2,1)} %reshape.82, bf16[512,768]{1,0:T(8,128)(2,1)S(1)} %bitcast.148), kind=kOutput, calls=%fused_computation.1 | convolution fusion | flops 3022848000 | bytes 16515072 | tf_op jit(solution)/shard_map/dot_general | solution.py:47
  168.2 14.8 %reshape.83 = f32[768,5,768]{2,1,0:T(8,128)} reshape(f32[3840,768]{1,0:T(8,128)} %convolution_multiply_fusion) | data formatting | bytes 23592960 | tf_op jit(solution)/shard_map/reshape | solution.py:148
  183.0 0.0 reduce-scatter.12.cloned.1.call-start
  183.1 2.4 collective-permute-start.2
  185.5 3.2 fusion.20
  188.8 2.1 collective-permute-start.3
  190.9 3.2 fusion.24
  194.2 99.7 %reduce-scatter.8.cloned.1.call-done = f32[48,5,768]{2,1,0:T(8,128)} async-done(((f32[768,5,768]{2,1,0:T(8,128)}), f32[48,5,768]{2,1,0:T(8,128)}) %reduce-scatter.8.cloned.1.call-update) | async-done | bytes 737296 | tf_op jit(solution)/shard_map/reduce_scatter | solution.py:149
  293.9 13.2 %copy.56 = f32[48,5,768]{1,0,2:T(8,128)} copy(f32[48,5,768]{2,1,0:T(8,128)} %reduce-scatter.8.cloned.1.call-done) | data formatting | bytes 1474560
  307.1 12.9 %reshape.87 = f32[768,240]{1,0:T(8,128)} reshape(f32[768,48,5]{2,1,0:T(8,128)} %bitcast.142) | data formatting | bytes 1474560
  319.9 2.1 fusion.28
  322.1 2.2 fusion.16
  324.3 3.3 multiply_reduce_fusion
  327.6 1.3 fusion.60
  328.9 195.8 %reduce-scatter.12.cloned.1.call-done = f32[48,240]{1,0:T(8,128)} async-done(((f32[768,240]{1,0:T(8,128)}), f32[48,240]{1,0:T(8,128)}) %reduce-scatter.12.cloned.1.call-update) | async-done | bytes 46096
  524.7 1.4 reshape.88
  526.1 1.2 copy.49
  (42 shorter events, 0.2 us)
Async XLA Ops:
  7.2 16.2 %copy-start = (bf16[768,768]{1,0:T(8,128)(2,1)S(1)}, bf16[768,768]{1,0:T(8,128)(2,1)}, u32[]{:S(2)}) copy-start(bf16[768,768]{1,0:T(8,128)(2,1)} %param.15) | copy-start | bytes 3538948
  7.2 147.8 %reduce-scatter.10.cloned.1.call-start = ((), (), s32[]{:S(2)}) async-start(), calls=%async_computation.4 | async-start | bytes 3342336
  10.4 9.5 %collective-permute-start = (bf16[1,2,768]{2,1,0:T(2,128)(2,1)S(1)}, bf16[1,2,768]{2,1,0:T(2,128)(2,1)S(1)}, u32[]{:S(2)}, u32[]{:S(2)}) collective-permute-start(bf16[1,2,768]{2,1,0:T(2,128)(2,1)S(1)} %get-tuple-element.8), channel_id=1, source_target_pairs={{0,1},{1,2},{2,3},{3,4},{4,5},{5,6},{6,7},{7,8},{8,9},{9,10},{10,1... | collective-permute-start | bytes 9224 | tf_op jit(solution)/shard_map/ppermute | solution.py:18
  12.3 6.4 %copy-start.8 = (bf16[768,768]{1,0:T(8,128)(2,1)S(1)}, bf16[768,768]{1,0:T(8,128)(2,1)}, u32[]{:S(2)}) copy-start(bf16[768,768]{1,0:T(8,128)(2,1)} %param.18) | copy-start | bytes 3538948
  12.3 6.4 %copy-start.12 = (bf16[1,32,768]{2,1,0:T(8,128)(2,1)S(1)}, bf16[1,32,768]{2,1,0:T(8,128)(2,1)}, u32[]{:S(2)}) copy-start(bf16[1,32,768]{2,1,0:T(8,128)(2,1)} %param.19) | copy-start | bytes 147460
  12.3 7.5 %copy-start.11 = (bf16[5,768,768]{2,1,0:T(8,128)(2,1)S(1)}, bf16[5,768,768]{2,1,0:T(8,128)(2,1)}, u32[]{:S(2)}) copy-start(bf16[5,768,768]{2,1,0:T(8,128)(2,1)} %param.14) | copy-start | bytes 17694724
  12.3 9.2 %collective-permute-start.1 = (bf16[1,2,768]{2,1,0:T(2,128)(2,1)S(1)}, bf16[1,2,768]{2,1,0:T(2,128)(2,1)S(1)}, u32[]{:S(2)}, u32[]{:S(2)}) collective-permute-start(bf16[1,2,768]{2,1,0:T(2,128)(2,1)S(1)} %get-tuple-element.9), channel_id=1, source_target_pairs={{1,0},{2,1},{3,2},{4,3},{5,4},{6,5},{7,6},{8,7},{9,8},{10,9},{11,1... | collective-permute-start | bytes 9224 | tf_op jit(solution)/shard_map/ppermute | solution.py:21
  19.9 0.8 copy-start.14
  22.3 2.1 copy-start.5
  23.4 1.9 copy-start.4
  48.4 3.1 copy-start.13
  49.8 0.8 copy-start.7
  81.9 2.3 copy-start.10
  81.9 2.7 copy-start.3
  83.5 0.7 copy-start.9
  90.2 0.7 copy-start.15
  90.2 203.6 %reduce-scatter.8.cloned.1.call-start = ((), (), s32[]{:S(2)}) async-start(), calls=%async_computation.3 | async-start | bytes 20054016 | tf_op jit(solution)/shard_map/reduce_scatter | solution.py:149
  105.3 8.5 %copy-start.2 = (bf16[512,768]{0,1:T(8,128)(2,1)S(1)}, bf16[512,768]{0,1:T(8,128)(2,1)}, u32[]{:S(2)}) copy-start(bf16[512,768]{0,1:T(8,128)(2,1)} %copy.36) | copy-start | bytes 2359300
  116.4 41.5 %copy-start.6 = (bf16[768,768]{1,0:T(8,128)(2,1)S(1)}, bf16[768,768]{1,0:T(8,128)(2,1)}, u32[]{:S(2)}) copy-start(bf16[768,768]{1,0:T(8,128)(2,1)} %param.17) | copy-start | bytes 3538948
  183.0 341.7 %reduce-scatter.12.cloned.1.call-start = ((), (), s32[]{:S(2)}) async-start(), calls=%async_computation.5 | async-start | bytes 835584
  183.1 7.8 %collective-permute-start.2 = (bf16[1,2,768]{2,1,0:T(2,128)(2,1)S(1)}, bf16[1,2,768]{2,1,0:T(2,128)(2,1)S(1)}, u32[]{:S(2)}, u32[]{:S(2)}) collective-permute-start(bf16[1,2,768]{2,1,0:T(2,128)(2,1)S(1)} %get-tuple-element.6), channel_id=1, source_target_pairs={{1,0},{2,1},{3,2},{4,3},{5,4},{6,5},{7,6},{8,7},{9,8},{10,9},{11,1... | collective-permute-start | bytes 9224 | tf_op jit(solution)/shard_map/ppermute | solution.py:21
  188.8 133.3 %collective-permute-start.3 = (bf16[1,2,768]{2,1,0:T(2,128)(2,1)S(1)}, bf16[1,2,768]{2,1,0:T(2,128)(2,1)S(1)}, u32[]{:S(2)}, u32[]{:S(2)}) collective-permute-start(bf16[1,2,768]{2,1,0:T(2,128)(2,1)S(1)} %get-tuple-element.7), channel_id=1, source_target_pairs={{0,1},{1,2},{2,3},{3,4},{4,5},{5,6},{6,7},{7,8},{8,9},{9,10},{10,1... | collective-permute-start | bytes 9224 | tf_op jit(solution)/shard_map/ppermute | solution.py:18
  322.0 2.3 copy-start.16
  322.0 2.3 copy-start.17
  327.6 199.7 %copy-start.1 = (bf16[768,768]{1,0:T(8,128)(2,1)S(1)}, bf16[768,768]{1,0:T(8,128)(2,1)}, u32[]{:S(2)}) copy-start(bf16[768,768]{1,0:T(8,128)(2,1)} %param.15) | copy-start | bytes 3538948
Sparse Core Ops, SparseCore 0:
  90.4 64.5 reduce-scatter.9
  183.2 110.6 reduce-scatter.7
  320.1 204.6 reduce-scatter.11
where the time goes:
time: 536 us; the launch traced here: 534 us
  waiting for transfers between devices  334 us (62%)
  local copies, waits for them, and re-layouts  71.8 us (13%)
  matrix products  48.2 us (9%)
  blocking collectives  43.3 us (8%)
  between operations  14.1 us (3%)
  other arithmetic  11.5 us (2%)
  starting transfers between devices  10.7 us (2%)
    unnamed x5, waiting for transfers between devices  234 us
    reduce_scatter x1, waiting for transfers between devices, per_device(): lax.psum_scatter(whole_terms, 'ctx', scatter_dimension=0, tiled=True)  99.7 us
    unnamed x42, local copies, waits for them, and re-layouts  35.3 us
    all_gather x1, blocking collectives, per_device(): lax.all_gather(values_local, 'ctx', axis=0, tiled=True)  22.8 us
    all_gather x1, blocking collectives, per_device(): lax.all_gather(keys_local, 'ctx', axis=0, tiled=True)  20.5 us
    dot_general x9, matrix products, dot_right_t(): lax.dot_general(left, right, (((1,), (1,)), ((), ())), preferred_element_...  18.7 us
    reshape x1, local copies, waits for them, and re-layouts, per_device(): (dot_left_t(windows, grad_rows) * factor).reshape(channels, kernel, chann...  14.8 us
  transfers between devices with their start and end apart: 7, of which 3 were waited for; matrix products, arithmetic and copies ran while one was open for 14% of the time, Pallas kernels for 0%

commit v1 on v0

--- a/solution.py
+++ b/solution.py
@@ -8,6 +8,13 @@
 EPSILON = 1e-06
 GELU_SCALE = 0.7978845608028654
 CUBIC = 0.044715
+
+
+def swapped_in(shard, axis, dim):
+    size = lax.axis_size(axis)
+    tiles = jnp.stack([shard for _ in range(size)])
+    tiles = lax.all_to_all(tiles, axis, split_axis=0, concat_axis=0)
+    return jnp.concatenate(tiles, axis=dim)
 
 
 def extended(block, sides, width):
@@ -83,7 +90,7 @@
     values_local = jnp.dot(pooled, w_value, preferred_element_type=jnp.float32).astype(jnp.bfloat16)
     keys_all, values_all = (
         lax.all_gather(keys_local, "ctx", axis=0, tiled=True),
-        lax.all_gather(values_local, "ctx", axis=0, tiled=True),
+        swapped_in(values_local, "ctx", 0),
     )
     scale = 1.0 / DH**0.5
     query_heads = heads_split(queries)

time: 536 us -> 530 us (0.989)
  blocking collectives: 43.3 us -> 20.5 us
  starting transfers between devices: 10.7 us -> 18.1 us
  waiting for transfers between devices: 334 us -> 341 us
    all_gather x1 -> x0, blocking collectives: 22.8 us -> none  [per_device(): lax.all_gather(values_local, 'ctx', axis=0, tiled=True)]
    all_to_all x0 -> x1, starting transfers between devices: none -> 7.41 us  [swapped_in(): tiles = lax.all_to_all(tiles, axis, split_axis=0, concat_axis=0)]
    unnamed x42 -> x40, local copies, waits for them, and re-layouts: 35.3 us -> 35.3 us
  transfers between devices with their start and end apart: 7 -> 8, of which waited for: 3 -> 4; matrix products, arithmetic and copies ran while one was open for 14% -> 15% of each run, Pallas kernels for 0% -> 0%
where the time goes in v1:
time: 530 us; the launch traced here: 528 us
  waiting for transfers between devices  341 us (64%)
  local copies, waits for them, and re-layouts  73.9 us (14%)
  matrix products  48.6 us (9%)
  blocking collectives  20.5 us (4%)
  starting transfers between devices  18.1 us (3%)
  between operations  14.1 us (3%)
  other arithmetic  11.6 us (2%)
    unnamed x5, waiting for transfers between devices  237 us
    reduce_scatter x1, waiting for transfers between devices, per_device(): lax.psum_scatter(whole_terms, 'ctx', scatter_dimension=0, tiled=True)  99.7 us
    unnamed x40, local copies, waits for them, and re-layouts  35.3 us
    all_gather x1, blocking collectives, per_device(): lax.all_gather(keys_local, 'ctx', axis=0, tiled=True)  20.5 us
    dot_general x9, matrix products, dot_right_t(): lax.dot_general(left, right, (((1,), (1,)), ((), ())), preferred_element_...  18.7 us
    reshape x1, local copies, waits for them, and re-layouts, per_device(): (dot_left_t(windows, grad_rows) * factor).reshape(channels, kernel, chann...  14.8 us
  transfers between devices with their start and end apart: 8, of which 4 were waited for; matrix products, arithmetic and copies ran while one was open for 15% of the time, Pallas kernels for 0%

profile of v1, /device:TPU:8, one launch (start us, length us, event | category | flops | bytes accessed | tf_op | source)
XLA Modules:
  0.0 527.9 jit_solution(12977875594865591700)
XLA Ops:
  7.2 0.8 convert_element_type.74
  8.0 1.7 multiply_reduce_fusion.1
  9.6 0.7 fusion.122
  10.3 1.9 collective-permute-start
  12.3 3.9 collective-permute-start.1
  16.2 2.5 fusion.22
  18.7 1.1 fusion.40
  19.8 0.8 fusion.26
  20.6 0.8 fusion.30
  21.5 0.8 fusion.18
  22.3 1.1 bitcast_reduce_fusion
  23.4 0.9 fusion.39
  24.3 0.9 convolution_convert_fusion.2
  25.3 0.3 convolution_convert_fusion.5
  25.6 20.5 %all_gather.3 = bf16[512,768]{1,0:T(8,128)(2,1)} all-gather(bf16[32,768]{1,0:T(8,128)(2,1)S(1)} %convolution_convert_fusion.5), channel_id=1, replica_groups=mesh['dp'=16,'ctx'=16] {'ctx'}, dimensions={0}, use_global_device_ids=true | all-gather | bytes 835584 | tf_op jit(solution)/shard_map/all_gather | solution.py:92
  46.0 2.3 copy.33
  48.3 1.8 stack.14
  50.1 7.4 %all-to-all-start = ((bf16[16,32,768]{2,1,0:T(8,128)(2,1)}), bf16[16,32,768]{2,1,0:T(8,128)(2,1)}, u32[]{:S(2)}, u32[]{:S(2)}) async-start(bf16[16,32,768]{2,1,0:T(8,128)(2,1)} %stack.14), calls=%async_computation | async-start | bytes 1572864 | tf_op jit(solution)/shard_map/all_to_all | solution.py:16
  57.5 0.0 reduce-scatter.10.cloned.1.call-start
  57.6 1.4 convolution_multiply_fusion.1
  59.0 0.7 copy-done.7
  59.7 0.9 fusion.102
  60.6 2.8 fusion.79
  63.5 3.9 all-to-all-done
  67.4 2.7 reshape_reshape.3
  70.1 2.6 fusion.38
  72.7 1.9 fusion.32
  74.6 0.7 copy-done.9
  75.3 0.4 fusion.82
  75.7 1.9 pad_maximum_fusion
  77.7 3.6 copy.48
  81.3 0.2 reduce-scatter.8.cloned.1.call-start
  81.6 0.4 copy-done.14
  82.0 1.1 bitcast_dynamic-update-slice_fusion.4
  83.0 1.1 bitcast_dynamic-update-slice_fusion.3
  84.1 1.6 bitcast_dynamic-update-slice_fusion.2
  85.7 1.2 bitcast_dynamic-update-slice_fusion.1
  86.9 1.1 bitcast_dynamic-update-slice_fusion
  87.9 8.4 %copy.44 = bf16[512,768,5]{0,2,1:T(8,128)(2,1)} copy(bf16[512,768,5]{1,0,2:T(8,128)(2,1)} %bitcast_dynamic-update-slice_fusion) | data formatting | bytes 7864320 | tf_op jit(solution)/shard_map/stack | solution.py:151
  96.4 8.5 %reshape.80 = bf16[512,3840]{0,1:T(8,128)(2,1)} reshape(bf16[512,768,5]{0,2,1:T(8,128)(2,1)} %copy.44) | data formatting | bytes 7864320 | tf_op jit(solution)/shard_map/reshape | solution.py:153
  104.9 1.3 fusion.41
  106.2 1.3 convolution_add_fusion.2
  107.5 41.6 %reduce-scatter.10.cloned.1.call-done = f32[32,1536]{1,0:T(8,128)} async-done(((f32[512,1536]{1,0:T(8,128)}), f32[32,1536]{1,0:T(8,128)}) %reduce-scatter.10.cloned.1.call-update) | async-done | bytes 196624
  149.1 1.1 copy.49
  150.3 1.7 convolution_add_fusion.1
  152.0 0.5 fusion.34
  152.5 0.1 broadcast_in_dim.7
  152.6 9.7 %convolution_multiply_fusion = f32[3840,768]{1,0:T(8,128)} fusion(bf16[512,3840]{0,1:T(8,128)(2,1)} %reshape.80, bf16[512,768]{1,0:T(8,128)(2,1)S(1)} %bitcast.145), kind=kOutput, calls=%fused_computation.1 | convolution fusion | flops 3022848000 | bytes 16515072 | tf_op jit(solution)/shard_map/dot_general | solution.py:54
  162.3 14.8 %reshape.81 = f32[768,5,768]{2,1,0:T(8,128)} reshape(f32[3840,768]{1,0:T(8,128)} %convolution_multiply_fusion) | data formatting | bytes 23592960 | tf_op jit(solution)/shard_map/reshape | solution.py:155
  177.2 0.0 reduce-scatter.12.cloned.1.call-start
  177.2 2.5 collective-permute-start.2
  179.7 3.2 fusion.20
  182.9 2.1 collective-permute-start.3
  185.1 3.2 fusion.24
  188.3 99.7 %reduce-scatter.8.cloned.1.call-done = f32[48,5,768]{2,1,0:T(8,128)} async-done(((f32[768,5,768]{2,1,0:T(8,128)}), f32[48,5,768]{2,1,0:T(8,128)}) %reduce-scatter.8.cloned.1.call-update) | async-done | bytes 737296 | tf_op jit(solution)/shard_map/reduce_scatter | solution.py:156
  288.0 13.1 %copy.50 = f32[48,5,768]{1,0,2:T(8,128)} copy(f32[48,5,768]{2,1,0:T(8,128)} %reduce-scatter.8.cloned.1.call-done) | data formatting | bytes 1474560
  301.1 12.9 %reshape.85 = f32[768,240]{1,0:T(8,128)} reshape(f32[768,48,5]{2,1,0:T(8,128)} %bitcast.139) | data formatting | bytes 1474560
  314.0 2.1 fusion.28
  316.2 2.2 fusion.16
  318.4 3.3 multiply_reduce_fusion
  321.7 1.3 fusion.60
  323.0 195.8 %reduce-scatter.12.cloned.1.call-done = f32[48,240]{1,0:T(8,128)} async-done(((f32[768,240]{1,0:T(8,128)}), f32[48,240]{1,0:T(8,128)}) %reduce-scatter.12.cloned.1.call-update) | async-done | bytes 46096
  518.8 1.4 reshape.86
  520.2 1.2 copy.45
  (42 shorter events, 0.2 us)
Async XLA Ops:
  7.2 16.2 %copy-start = (bf16[768,768]{1,0:T(8,128)(2,1)S(1)}, bf16[768,768]{1,0:T(8,128)(2,1)}, u32[]{:S(2)}) copy-start(bf16[768,768]{1,0:T(8,128)(2,1)} %param.15) | copy-start | bytes 3538948
  10.3 9.5 %collective-permute-start = (bf16[1,2,768]{2,1,0:T(2,128)(2,1)S(1)}, bf16[1,2,768]{2,1,0:T(2,128)(2,1)S(1)}, u32[]{:S(2)}, u32[]{:S(2)}) collective-permute-start(bf16[1,2,768]{2,1,0:T(2,128)(2,1)S(1)} %get-tuple-element.8), channel_id=1, source_target_pairs={{0,1},{1,2},{2,3},{3,4},{4,5},{5,6},{6,7},{7,8},{8,9},{9,10},{10,1... | collective-permute-start | bytes 9224 | tf_op jit(solution)/shard_map/ppermute | solution.py:25
  12.3 6.4 %copy-start.8 = (bf16[768,768]{1,0:T(8,128)(2,1)S(1)}, bf16[768,768]{1,0:T(8,128)(2,1)}, u32[]{:S(2)}) copy-start(bf16[768,768]{1,0:T(8,128)(2,1)} %param.18) | copy-start | bytes 3538948
  12.3 6.4 %copy-start.12 = (bf16[1,32,768]{2,1,0:T(8,128)(2,1)S(1)}, bf16[1,32,768]{2,1,0:T(8,128)(2,1)}, u32[]{:S(2)}) copy-start(bf16[1,32,768]{2,1,0:T(8,128)(2,1)} %param.19) | copy-start | bytes 147460
  12.3 7.5 %copy-start.11 = (bf16[5,768,768]{2,1,0:T(8,128)(2,1)S(1)}, bf16[5,768,768]{2,1,0:T(8,128)(2,1)}, u32[]{:S(2)}) copy-start(bf16[5,768,768]{2,1,0:T(8,128)(2,1)} %param.14) | copy-start | bytes 17694724
  12.3 9.2 %collective-permute-start.1 = (bf16[1,2,768]{2,1,0:T(2,128)(2,1)S(1)}, bf16[1,2,768]{2,1,0:T(2,128)(2,1)S(1)}, u32[]{:S(2)}, u32[]{:S(2)}) collective-permute-start(bf16[1,2,768]{2,1,0:T(2,128)(2,1)S(1)} %get-tuple-element.9), channel_id=1, source_target_pairs={{1,0},{2,1},{3,2},{4,3},{5,4},{6,5},{7,6},{8,7},{9,8},{10,9},{11,1... | collective-permute-start | bytes 9224 | tf_op jit(solution)/shard_map/ppermute | solution.py:28
  19.8 0.8 copy-start.13
  22.3 2.1 copy-start.5
  23.4 1.9 copy-start.4
  50.1 17.3 %all-to-all-start = ((bf16[16,32,768]{2,1,0:T(8,128)(2,1)}), bf16[16,32,768]{2,1,0:T(8,128)(2,1)}, u32[]{:S(2)}, u32[]{:S(2)}) async-start(bf16[16,32,768]{2,1,0:T(8,128)(2,1)} %stack.14), calls=%async_computation | async-start | bytes 1572864 | tf_op jit(solution)/shard_map/all_to_all | solution.py:16
  57.5 91.6 %reduce-scatter.10.cloned.1.call-start = ((), (), s32[]{:S(2)}) async-start(), calls=%async_computation.5 | async-start | bytes 3342336
  59.0 0.7 copy-start.7
  72.7 2.6 copy-start.10
  72.7 3.0 copy-start.3
  74.6 0.7 copy-start.9
  81.3 0.7 copy-start.14
  81.3 206.7 %reduce-scatter.8.cloned.1.call-start = ((), (), s32[]{:S(2)}) async-start(), calls=%async_computation.4 | async-start | bytes 20054016 | tf_op jit(solution)/shard_map/reduce_scatter | solution.py:156
  96.4 8.5 %copy-start.2 = (bf16[512,768]{0,1:T(8,128)(2,1)S(1)}, bf16[512,768]{0,1:T(8,128)(2,1)}, u32[]{:S(2)}) copy-start(bf16[512,768]{0,1:T(8,128)(2,1)} %copy.33) | copy-start | bytes 2359300
  107.5 44.6 %copy-start.6 = (bf16[768,768]{1,0:T(8,128)(2,1)S(1)}, bf16[768,768]{1,0:T(8,128)(2,1)}, u32[]{:S(2)}) copy-start(bf16[768,768]{1,0:T(8,128)(2,1)} %param.17) | copy-start | bytes 3538948
  177.2 341.7 %reduce-scatter.12.cloned.1.call-start = ((), (), s32[]{:S(2)}) async-start(), calls=%async_computation.6 | async-start | bytes 835584
  177.2 7.9 %collective-permute-start.2 = (bf16[1,2,768]{2,1,0:T(2,128)(2,1)S(1)}, bf16[1,2,768]{2,1,0:T(2,128)(2,1)S(1)}, u32[]{:S(2)}, u32[]{:S(2)}) collective-permute-start(bf16[1,2,768]{2,1,0:T(2,128)(2,1)S(1)} %get-tuple-element.6), channel_id=1, source_target_pairs={{1,0},{2,1},{3,2},{4,3},{5,4},{6,5},{7,6},{8,7},{9,8},{10,9},{11,1... | collective-permute-start | bytes 9224 | tf_op jit(solution)/shard_map/ppermute | solution.py:28
  182.9 133.2 %collective-permute-start.3 = (bf16[1,2,768]{2,1,0:T(2,128)(2,1)S(1)}, bf16[1,2,768]{2,1,0:T(2,128)(2,1)S(1)}, u32[]{:S(2)}, u32[]{:S(2)}) collective-permute-start(bf16[1,2,768]{2,1,0:T(2,128)(2,1)S(1)} %get-tuple-element.7), channel_id=1, source_target_pairs={{0,1},{1,2},{2,3},{3,4},{4,5},{5,6},{6,7},{7,8},{8,9},{9,10},{10,1... | collective-permute-start | bytes 9224 | tf_op jit(solution)/shard_map/ppermute | solution.py:25
  316.1 2.3 copy-start.15
  316.1 2.3 copy-start.16
  321.7 199.7 %copy-start.1 = (bf16[768,768]{1,0:T(8,128)(2,1)S(1)}, bf16[768,768]{1,0:T(8,128)(2,1)}, u32[]{:S(2)}) copy-start(bf16[768,768]{1,0:T(8,128)(2,1)} %param.15) | copy-start | bytes 3538948
Sparse Core Ops, SparseCore 0:
  81.4 67.6 reduce-scatter.9
  177.3 110.6 reduce-scatter.7
  314.1 204.6 reduce-scatter.11
